TPU v7x, 128 devices: a whole 4x4x4 slice. The times are simulated.
128 devices in a mesh: wide: 16 (over x, z), narrow: 8 (over y, core).
Axes of the slice: x: 4, y: 4, z: 4, core: 2. Of those that a mesh axis runs over, the one named last changes fastest.
Arguments:
- activations: bfloat16 [4096, 16384], P('wide', 'narrow'), may hold values from -6 to 6
- grad_out: bfloat16 [4096, 8192], P('narrow', 'wide'), may hold values from -0.09375 to 0.09375
- momentum: float32 [8192, 16384], P('wide', 'narrow'), may hold values from -90 to 90
- right_factor: float32 [16384, 512], P('narrow'), may hold values from -0.046875 to 0.046875
Outputs:
- new_momentum: float32 [8192, 16384], P('wide', 'narrow')
- new_right: float32 [16384, 512], P('narrow')
- update: bfloat16 [8192, 16384], P('wide', 'narrow')
All inputs are finite; a program needn't handle non-finite values.
Results may differ from a plain program's by a relative error of at most 0.0012.
Values may be sent and summed in bfloat16 or wider, within the bound.
A program may use at most 128 MiB of HBM per device.

v0:
```python
import math
import jax
import jax.numpy as jnp
from jax import lax
from jax.sharding import Mesh
from jax.sharding import PartitionSpec as P

DOUT = 8192
DIN = 16384
RANK = 512
NARROW = ("narrow_0", "narrow_1")
WIDE = ("wide_0", "wide_1")
FEEDBACK = 0.05
EPSILON = 1e-06


def sent_to_all(array, axis):
    devices = lax.axis_size(axis)
    return lax.all_to_all(
        jnp.broadcast_to(array[None], (devices, *array.shape)), axis, 0, 0, tiled=True
    )


def laid_out(tiles, dim):
    tiles = jnp.moveaxis(tiles, 0, dim)
    lengths = tiles.shape
    return tiles.reshape(*lengths[:dim], lengths[dim] * lengths[dim + 1], *lengths[dim + 2 :])


def gathered_by_axis(array, axes, dim):
    far, near = axes
    tiles = sent_to_all(sent_to_all(array, far), near)
    return laid_out(tiles.swapaxes(0, 1).reshape(-1, *array.shape), dim)


def split_up(array, dim, devices):
    before, after = (array.shape[:dim], array.shape[dim + 1 :])
    return jnp.moveaxis(array.reshape(*before, devices, -1, *after), dim, 0)


def summed_on_arrival(array, axis, dim):
    tiles = split_up(array, dim, lax.axis_size(axis))
    arrived = lax.all_to_all(tiles, axis, split_axis=0, concat_axis=0, tiled=True)
    return arrived.sum(axis=0)


def padded_to(lines, devices):
    spare = -len(lines) % devices
    return jnp.pad(lines, [(0, spare)] + [(0, 0)] * (lines.ndim - 1))


def summed_rows(array, axes, dim):
    far, near = axes
    own = summed_on_arrival(split_up(array, dim, lax.axis_size(far)), near, dim + 1)
    return jnp.sum(lax.all_to_all(own, far, 0, 0, tiled=True), axis=0)


def total_of(array, axes):
    lines = array.reshape(-1, array.shape[-1])
    padded = padded_to(lines, lax.axis_size(axes[0]) * lax.axis_size(axes[1]))
    whole = gathered_by_axis(summed_rows(padded, axes, 0), axes, 0)
    return lax.slice_in_dim(whole, 0, len(lines)).reshape(array.shape)


def gathered_copies(array, axis, dim):
    return laid_out(sent_to_all(array, axis), dim)


def own_rows(total, axes):
    for axis in axes:
        total = lax.psum_scatter(total, axis, scatter_dimension=0, tiled=True)
    return total


def taken_together(array, axis):
    return sent_to_all(array, axis).sum(axis=0)


def over_axes(array, axes):
    far, near = axes
    nearer = taken_together(array, near)
    return taken_together(nearer, far)


def body(activations, grad_out, momentum, right_factor):
    highest = lax.Precision.HIGHEST
    out_rows = gathered_by_axis(grad_out, ("narrow_0", "narrow_1"), 0)
    gradient = lax.dot_general(
        out_rows,
        lax.all_gather(activations, WIDE, axis=0, tiled=True),
        (((0,), (0,)), ((), ())),
        preferred_element_type=jnp.float32,
    )
    buffer = momentum + gradient
    left_share = summed_on_arrival(
        jnp.dot(buffer, right_factor, precision=highest, preferred_element_type=jnp.float32),
        NARROW,
        0,
    )
    gram_local = jnp.dot(
        left_share.T, left_share, precision=highest, preferred_element_type=jnp.float32
    )
    gram_matrix = total_of(gram_local, (("wide_0", "wide_1", "narrow_0"), "narrow_1"))
    lower_factor = jnp.linalg.cholesky(gram_matrix)
    ortho_share = jax.scipy.linalg.solve_triangular(lower_factor, left_share.T, lower=True).T
    ortho_left = gathered_copies(ortho_share, NARROW, 0)
    right_share = own_rows(
        lax.dot_general(
            buffer,
            ortho_left,
            (((0,), (0,)), ((), ())),
            precision=highest,
            preferred_element_type=jnp.float32,
        ),
        WIDE,
    )
    col_squares = over_axes(
        jnp.sum(right_share * right_share, axis=0), (("wide_0", "wide_1", "narrow_0"), "narrow_1")
    )
    right_raw = lax.all_gather(right_share, WIDE, axis=0, tiled=True)
    feedback = lax.dot_general(
        ortho_left,
        right_raw,
        (((1,), (1,)), ((), ())),
        precision=highest,
        preferred_element_type=jnp.float32,
    )
    new_momentum = buffer - FEEDBACK * feedback
    new_right = right_raw / (jnp.sqrt(col_squares) + EPSILON)
    update_scale = math.sqrt(DOUT * DIN / RANK)
    product = lax.dot_general(
        ortho_left,
        new_right,
        (((1,), (1,)), ((), ())),
        precision=highest,
        preferred_element_type=jnp.float32,
    )
    update = (update_scale * product).astype(jnp.bfloat16)
    return (new_momentum, new_right, update)


def solution(mesh):
    finer = Mesh(mesh.devices.reshape(4, 4, 4, 2), ("wide_0", "wide_1", "narrow_0", "narrow_1"))
    in_specs = (P(WIDE, NARROW), P(NARROW, WIDE), P(WIDE, NARROW), P(NARROW, None))
    out_specs = (P(WIDE, NARROW), P(NARROW, None), P(WIDE, NARROW))
    return jax.shard_map(body, mesh=finer, in_specs=in_specs, out_specs=out_specs, check_vma=False)
```

profile of v0, /device:TPU:1, one launch (start us, length us, event | category | flops | bytes accessed | tf_op | source)
XLA Modules:
  0.0 525.0 jit_solution(6163401556393695659)
XLA Ops:
  9.1 30.2 %all_to_all.52 = bf16[4,512,512]{2,1,0:T(8,128)(2,1)S(1)} all-to-all(bf16[4,512,512]{2,1,0:T(8,128)(2,1)S(1)} %broadcast_in_dim.15), channel_id=1, replica_groups=mesh['wide_0'=4,'wide_1'=4,'narrow_0'=4,'narrow_1'=2] {'narrow_0'}, dimensions={0} | all-to-all | bytes 4194304 | tf_op jit(solution)/shard_map/all_to_all | solution.py:19
  39.7 8.6 %all_to_all.53 = bf16[2,4,512,512]{3,2,1,0:T(8,128)(2,1)S(1)} all-to-all(bf16[2,4,512,512]{3,2,1,0:T(8,128)(2,1)S(1)} %broadcast_in_dim.16), channel_id=1, replica_groups=mesh['wide_0'=4,'wide_1'=4,'narrow_0'=4,'narrow_1'=2] {'narrow_1'}, dimensions={0} | all-to-all | bytes 8388608 | tf_op jit(solution)/shard_map/all_to_all | solution.py:19
  50.8 74.0 %all-gather.3.cloned.1.call-done = bf16[4096,2048]{1,0:T(8,128)(2,1)} async-done(((bf16[256,2048]{1,0:T(8,128)(2,1)}), bf16[4096,2048]{1,0:T(8,128)(2,1)}) %all-gather.3.cloned.1.call-update) | async-done | bytes 16777232 | tf_op jit(solution)/shard_map/all_gather | solution.py:90
  124.8 14.4 %convolution_add_fusion = f32[512,2048]{1,0:T(8,128)S(1)} fusion(f32[512,2048]{1,0:T(8,128)} %param.6, bf16[4096,512]{1,0:T(8,128)(2,1)} %bitcast.79, bf16[4096,2048]{1,0:T(8,128)(2,1)} %all-gather.3.cloned.1.call-done), kind=kOutput, calls=%fused_computation.4 | convolution fusion | flops 8590983168 | bytes 29360128 | tf_op jit(solution)/shard_map/dot_general | solution.py:88
  146.1 19.9 %all_to_all.54 = f32[8,64,512]{2,1,0:T(8,128)S(1)} all-to-all(f32[8,64,512]{2,1,0:T(8,128)S(1)} %bitcast.78), channel_id=1, replica_groups=mesh['wide_0'=4,'wide_1'=4,'narrow_0'=4,'narrow_1'=2] {'narrow_0','narro..., dimensions={0} | all-to-all | bytes 2097152 | tf_op jit(solution)/shard_map/all_to_all | solution.py:43
  172.9 18.3 %all_to_all.56 = f32[64,4,512]{2,1,0:T(4,128)S(1)} all-to-all(f32[64,4,512]{2,1,0:T(4,128)S(1)} %copy.31), channel_id=1, replica_groups=mesh['wide_0'=4,'wide_1'=4,'narrow_0'=4,'narrow_1'=2] {'wide_0','wide_1'..., dimensions={0} | all-to-all | bytes 1048576 | tf_op jit(solution)/shard_map/all_to_all | solution.py:55
  197.1 10.7 %all-to-all-done.5 = f32[64,4,512]{2,1,0:T(4,128)S(1)} async-done(((f32[64,4,512]{2,1,0:T(4,128)}), f32[64,4,512]{2,1,0:T(4,128)S(1)}, u32[]{:S(2)}, u32[]{:S(2)}) %all-to-all-start.5) | async-done | bytes 524320 | tf_op jit(solution)/shard_map/all_to_all | solution.py:19
  216.5 11.7 %cholesky.104 = f32[128,128]{1,0:T(8,128)S(1)} custom-call(f32[128,128]{1,0:T(8,128)S(1)} %cholesky.266), custom_call_target="Cholesky" | custom-call | tf_op jit(solution)/shard_map/jit(cholesky)/cholesky | solution.py:104
  228.4 9.8 %custom-call.31 = f32[1,128,128]{1,2,0:T(8,128)S(1)} custom-call(f32[1,128,128]{2,1,0:T(8,128)S(1)} %get-tuple-element.30), custom_call_target="InvertDiagBlocksLowerTriangular" | custom-call | tf_op jit(solution)/shard_map/jit(cholesky)/cholesky | solution.py:104
  238.9 11.7 %cholesky.217 = f32[128,128]{1,0:T(8,128)S(1)} custom-call(f32[128,128]{1,0:T(8,128)S(1)} %cholesky.270), custom_call_target="Cholesky" | custom-call | tf_op jit(solution)/shard_map/jit(cholesky)/cholesky | solution.py:104
  250.7 10.0 %custom-call.32 = f32[1,128,128]{1,2,0:T(8,128)S(1)} custom-call(f32[1,128,128]{2,1,0:T(8,128)S(1)} %get-tuple-element.27), custom_call_target="InvertDiagBlocksLowerTriangular" | custom-call | tf_op jit(solution)/shard_map/jit(cholesky)/cholesky | solution.py:104
  261.3 11.7 %cholesky.238 = f32[128,128]{1,0:T(8,128)S(1)} custom-call(f32[128,128]{1,0:T(8,128)S(1)} %cholesky.275), custom_call_target="Cholesky" | custom-call | tf_op jit(solution)/shard_map/jit(cholesky)/cholesky | solution.py:104
  273.8 9.8 %custom-call.33 = f32[1,128,128]{1,2,0:T(8,128)S(1)} custom-call(f32[1,128,128]{2,1,0:T(8,128)S(1)} %get-tuple-element.24), custom_call_target="InvertDiagBlocksLowerTriangular" | custom-call | tf_op jit(solution)/shard_map/jit(cholesky)/cholesky | solution.py:104
  284.2 11.9 %cholesky.255 = f32[128,128]{1,0:T(8,128)S(1)} custom-call(f32[128,128]{1,0:T(8,128)S(1)} %convolution_subtract_fusion.2), custom_call_target="Cholesky" | custom-call | tf_op jit(solution)/shard_map/jit(cholesky)/cholesky | solution.py:104
  300.1 8.5 %while.1 = (s32[]{:T(128)}, f32[512,512]{1,0:T(8,128)S(1)}, s32[4,2]{0,1:T(2,128)S(1)}, f32[4,128,128]{2,1,0:T(8,128)S(1)}, s32[]{:T(128)}) while((s32[]{:T(128)}, f32[512,512]{1,0:T(8,128)S(1)}, s32[4,2]{0,1:T(2,128)S(1)}, f32[4,128,128]{2,1,0:T(8,128)S(1)}, s32[]{:T(128)}) %tuple.31), condition=%wide.while_cond, body=%wide.while_body.sunk | while | flops 2 | bytes 131181 | solution.py:105
  308.6 39.3 %custom-call.34 = f32[4,128,128]{1,2,0:T(8,128)S(1)} custom-call(f32[4,128,128]{2,1,0:T(8,128)S(1)} %get-tuple-element.10), custom_call_target="InvertDiagBlocksLowerTriangular" | custom-call | tf_op jit(solution)/shard_map/jit(_solve_triangular)/triangular_solve | solution.py:105
  349.7 17.9 %all_to_all.58 = f32[8,64,512]{2,1,0:T(8,128)S(1)} all-to-all(f32[8,64,512]{2,1,0:T(8,128)S(1)} %broadcast_in_dim.20), channel_id=1, replica_groups=mesh['wide_0'=4,'wide_1'=4,'narrow_0'=4,'narrow_1'=2] {'narrow_0','narro..., dimensions={0} | all-to-all | bytes 2097152 | tf_op jit(solution)/shard_map/all_to_all | solution.py:19
  367.6 8.4 %fusion.34 = f32[2048,512]{1,0:T(8,128)} fusion(f32[512,2048]{1,0:T(8,128)S(1)} %copy-done.1, f32[512,512]{1,0:T(8,128)S(1)} %bitcast.75), kind=kOutput, calls=%fused_computation.77 | convolution fusion | flops 6442450944 | bytes 9437184 | tf_op jit(solution)/shard_map/dot_general | solution.py:108
  376.0 43.0 %reduce-scatter.3.cloned.1.call-done = f32[512,512]{1,0:T(8,128)} async-done(((f32[2048,512]{1,0:T(8,128)}), f32[512,512]{1,0:T(8,128)}) %reduce-scatter.3.cloned.1.call-update) | async-done | bytes 1048592 | tf_op jit(solution)/shard_map/reduce_scatter | solution.py:71
  419.1 24.2 %reduce-scatter.5.cloned.1.call-done = f32[128,512]{1,0:T(8,128)} async-done(((f32[512,512]{1,0:T(8,128)}), f32[128,512]{1,0:T(8,128)}) %reduce-scatter.5.cloned.1.call-update) | async-done | bytes 262160 | tf_op jit(solution)/shard_map/reduce_scatter | solution.py:71
  450.2 17.3 %all_to_all.60 = f32[64,1,512]{2,1,0:T(1,128)S(1)} all-to-all(f32[64,1,512]{2,1,0:T(1,128)S(1)} %broadcast_in_dim.22), channel_id=1, replica_groups=mesh['wide_0'=4,'wide_1'=4,'narrow_0'=4,'narrow_1'=2] {'wide_0','wide_1'..., dimensions={0} | all-to-all | bytes 262144 | tf_op jit(solution)/shard_map/all_to_all | solution.py:19
  467.6 31.0 %all-gather.5.cloned.1.call-done = f32[2048,512]{1,0:T(8,128)} async-done(((f32[128,512]{1,0:T(8,128)}), f32[2048,512]{1,0:T(8,128)}) %all-gather.5.cloned.1.call-update) | async-done | bytes 4194320 | tf_op jit(solution)/shard_map/all_gather | solution.py:120
  501.4 8.1 %multiply_convert_fusion = bf16[512,2048]{1,0:T(8,128)(2,1)} fusion(f32[512,512]{1,0:T(8,128)S(1)} %bitcast.76, f32[2048,512]{1,0:T(8,128)S(1)} %broadcast_divide_fusion), kind=kOutput, calls=%fused_computation.2 | convolution fusion | flops 6444548096 | bytes 7340032 | tf_op jit(solution)/shard_map/dot_general | solution.py:131
  509.5 8.5 %multiply_subtract_fusion = f32[512,2048]{1,0:T(8,128)} fusion(f32[512,2048]{1,0:T(8,128)S(1)} %copy-done.2, f32[512,512]{1,0:T(8,128)S(1)} %bitcast.77, f32[2048,512]{1,0:T(8,128)S(1)} %copy-done.3), kind=kOutput, calls=%fused_computation.3 | convolution fusion | flops 6444548096 | bytes 13631488 | tf_op jit(solution)/shard_map/dot_general | solution.py:121
  (89 shorter events, 57.4 us)
Async XLA Ops:
  7.2 117.7 %all-gather.3.cloned.1.call-start = ((), (), s32[]{:S(2)}) async-start(), calls=%async_computation.12 | async-start | bytes 17825792 | tf_op jit(solution)/shard_map/all_gather | solution.py:90
  124.8 14.4 %copy-start.4 = (f32[2048,512]{1,0:T(8,128)S(1)}, f32[2048,512]{1,0:T(8,128)}, u32[]{:S(2)}) copy-start(f32[2048,512]{1,0:T(8,128)} %param.7) | copy-start | bytes 12582916
  139.2 6.9 %copy-start = (f32[512,2048]{1,0:T(8,128)}, f32[512,2048]{1,0:T(8,128)S(1)}, u32[]{:S(2)}) copy-start(f32[512,2048]{1,0:T(8,128)S(1)} %convolution_add_fusion) | copy-start | bytes 12582916
  192.1 15.8 %all-to-all-start.5 = ((f32[64,4,512]{2,1,0:T(4,128)}), f32[64,4,512]{2,1,0:T(4,128)S(1)}, u32[]{:S(2)}, u32[]{:S(2)}) async-start(f32[64,4,512]{2,1,0:T(4,128)} %broadcast_in_dim.18), calls=%async_computation.5 | async-start | bytes 1048576 | tf_op jit(solution)/shard_map/all_to_all | solution.py:19
  197.0 222.0 %reduce-scatter.3.cloned.1.call-start = ((), (), s32[]{:S(2)}) async-start(), calls=%async_computation.13 | async-start | bytes 5242880 | tf_op jit(solution)/shard_map/reduce_scatter | solution.py:71
  347.9 19.7 %copy-start.1 = (f32[512,2048]{1,0:T(8,128)S(1)}, f32[512,2048]{1,0:T(8,128)}, u32[]{:S(2)}) copy-start(f32[512,2048]{1,0:T(8,128)} %copy-done) | copy-start | bytes 12582916
  376.0 67.3 %reduce-scatter.5.cloned.1.call-start = ((), (), s32[]{:S(2)}) async-start(), calls=%async_computation.14 | async-start | bytes 1310720 | tf_op jit(solution)/shard_map/reduce_scatter | solution.py:71
  419.1 79.6 %all-gather.5.cloned.1.call-start = ((), (), s32[]{:S(2)}) async-start(), calls=%async_computation.15 | async-start | bytes 4456448 | tf_op jit(solution)/shard_map/all_gather | solution.py:120
  501.4 8.2 %copy-start.5 = (f32[2048,512]{1,0:T(8,128)}, f32[2048,512]{1,0:T(8,128)S(1)}, u32[]{:S(2)}) copy-start(f32[2048,512]{1,0:T(8,128)S(1)} %broadcast_divide_fusion) | copy-start | bytes 12582916
  501.4 8.2 %copy-start.2 = (f32[512,2048]{1,0:T(8,128)S(1)}, f32[512,2048]{1,0:T(8,128)}, u32[]{:S(2)}) copy-start(f32[512,2048]{1,0:T(8,128)} %copy-done) | copy-start | bytes 12582916
  501.4 8.2 %copy-start.3 = (f32[2048,512]{1,0:T(8,128)S(1)}, f32[2048,512]{1,0:T(8,128)}, u32[]{:S(2)}) copy-start(f32[2048,512]{1,0:T(8,128)} %all-gather.5.cloned.1.call-done) | copy-start | bytes 12582916
Sparse Core Ops, SparseCore 0:
  10.1 114.6 all-gather.2
  376.1 42.8 reduce-scatter.2
  421.6 21.6 reduce-scatter.4
  445.3 53.2 all-gather.4
where the time goes:
time: 536 us; the launch traced here: 525 us
  waiting for transfers between devices  184 us (34%)
  blocking collectives  131 us (24%)
  other arithmetic  123 us (23%)
  matrix products  50.7 us (9%)
  between operations  17.1 us (3%)
  local copies, waits for them, and re-layouts  15.1 us (3%)
    all_to_all x6, blocking collectives, sent_to_all(): lax.all_to_all(jnp.broadcast_to(array[None], (devices, *array.shape)), ax...  87.2 us
    another operation x14, other arithmetic, body(): lower_factor = jnp.linalg.cholesky(gram_matrix)  78.8 us
    all_gather x1, waiting for transfers between devices, body(): lax.all_gather(activations, WIDE, axis=0, tiled=True)  74 us
    reduce_scatter x2, waiting for transfers between devices, own_rows(): total = lax.psum_scatter(total, axis, scatter_dimension=0, tiled=True)  67.2 us
    another operation x3, other arithmetic, body(): jax.scipy.linalg.solve_triangular(lower_factor, left_share.T, lower=True)  39.4 us
    all_gather x1, waiting for transfers between devices, body(): right_raw = lax.all_gather(right_share, WIDE, axis=0, tiled=True)  31 us
    all_to_all x2, blocking collectives, summed_on_arrival(): lax.all_to_all(tiles, axis, split_axis=0, concat_axis=0, tiled=True)  25.1 us
    all_to_all x1, blocking collectives, summed_rows(): return jnp.sum(lax.all_to_all(own, far, 0, 0, tiled=True), axis=0)  18.3 us
  transfers between devices with their start and end apart: 5, of which 5 were waited for; matrix products, arithmetic and copies ran while one was open for 1% of the time, Pallas kernels for 0%

commit v1 on v0

--- a/solution.py
+++ b/solution.py
@@ -117,7 +117,9 @@
     col_squares = over_axes(
         jnp.sum(right_share * right_share, axis=0), (("wide_0", "wide_1", "narrow_0"), "narrow_1")
     )
-    right_raw = lax.all_gather(right_share, WIDE, axis=0, tiled=True)
+    right_raw = jnp.concatenate(
+        lax.all_to_all(jnp.stack([right_share] * lax.axis_size(WIDE)), WIDE, 0, 0), axis=0
+    )
     feedback = lax.dot_general(
         ortho_left,
         right_raw,

time: 536 us -> 575 us (1.073)
  the two profiles are of different devices: /device:TPU:1 before, /device:TPU:116 now
where the time goes in v1:
time: 575 us; the launch traced here: 564 us
  waiting for transfers between devices  212 us (37%)
  other arithmetic  128 us (22%)
  blocking collectives  118 us (21%)
  matrix products  52.3 us (9%)
  starting transfers between devices  18.7 us (3%)
  local copies, waits for them, and re-layouts  18.6 us (3%)
  between operations  17.1 us (3%)
    another operation x14, other arithmetic, body(): lower_factor = jnp.linalg.cholesky(gram_matrix)  78.8 us
    all_to_all x6, blocking collectives, sent_to_all(): lax.all_to_all(jnp.broadcast_to(array[None], (devices, *array.shape)), ax...  76.7 us
    all_gather x1, waiting for transfers between devices, body(): lax.all_gather(activations, WIDE, axis=0, tiled=True)  73.7 us
    reduce_scatter x2, waiting for transfers between devices, own_rows(): total = lax.psum_scatter(total, axis, scatter_dimension=0, tiled=True)  72.5 us
    all_to_all x1, waiting for transfers between devices, body(): lax.all_to_all(jnp.stack([right_share] * lax.axis_size(WIDE)), WIDE, 0, 0)  58.4 us
    another operation x3, other arithmetic, body(): jax.scipy.linalg.solve_triangular(lower_factor, left_share.T, lower=True)  39.4 us
    all_to_all x2, blocking collectives, summed_on_arrival(): lax.all_to_all(tiles, axis, split_axis=0, concat_axis=0, tiled=True)  22.1 us
    all_to_all x1, blocking collectives, summed_rows(): return jnp.sum(lax.all_to_all(own, far, 0, 0, tiled=True), axis=0)  19.1 us
  transfers between devices with their start and end apart: 5, of which 5 were waited for; matrix products, arithmetic and copies ran while one was open for 1% of the time, Pallas kernels for 0%

profile of v1, /device:TPU:116, one launch (start us, length us, event | category | flops | bytes accessed | tf_op | source)
XLA Modules:
  0.0 564.2 jit_solution(1806415406722532986)
XLA Ops:
  9.1 28.2 %all_to_all.57 = bf16[4,512,512]{2,1,0:T(8,128)(2,1)S(1)} all-to-all(bf16[4,512,512]{2,1,0:T(8,128)(2,1)S(1)} %broadcast_in_dim.15), channel_id=1, replica_groups=mesh['wide_0'=4,'wide_1'=4,'narrow_0'=4,'narrow_1'=2] {'narrow_0'}, dimensions={0} | all-to-all | bytes 4194304 | tf_op jit(solution)/shard_map/all_to_all | solution.py:19
  47.3 73.7 %all-gather.2.cloned.1.call-done = bf16[4096,2048]{1,0:T(8,128)(2,1)} async-done(((bf16[256,2048]{1,0:T(8,128)(2,1)}), bf16[4096,2048]{1,0:T(8,128)(2,1)}) %all-gather.2.cloned.1.call-update) | async-done | bytes 16777232 | tf_op jit(solution)/shard_map/all_gather | solution.py:90
  120.9 14.4 %convolution_add_fusion = f32[512,2048]{1,0:T(8,128)S(1)} fusion(f32[512,2048]{1,0:T(8,128)} %param.6, bf16[4096,512]{1,0:T(8,128)(2,1)} %bitcast.83, bf16[4096,2048]{1,0:T(8,128)(2,1)} %all-gather.2.cloned.1.call-done), kind=kOutput, calls=%fused_computation.4 | convolution fusion | flops 8590983168 | bytes 29360128 | tf_op jit(solution)/shard_map/dot_general | solution.py:88
  142.2 17.5 %all_to_all.59 = f32[8,64,512]{2,1,0:T(8,128)S(1)} all-to-all(f32[8,64,512]{2,1,0:T(8,128)S(1)} %bitcast.81), channel_id=1, replica_groups=mesh['wide_0'=4,'wide_1'=4,'narrow_0'=4,'narrow_1'=2] {'narrow_0','narro..., dimensions={0} | all-to-all | bytes 2097152 | tf_op jit(solution)/shard_map/all_to_all | solution.py:43
  166.0 19.1 %all_to_all.61 = f32[64,4,512]{2,1,0:T(4,128)S(1)} all-to-all(f32[64,4,512]{2,1,0:T(4,128)S(1)} %copy.31), channel_id=1, replica_groups=mesh['wide_0'=4,'wide_1'=4,'narrow_0'=4,'narrow_1'=2] {'wide_0','wide_1'..., dimensions={0} | all-to-all | bytes 1048576 | tf_op jit(solution)/shard_map/all_to_all | solution.py:55
  186.0 10.2 %all-to-all-start.5 = ((f32[64,4,512]{2,1,0:T(4,128)}), f32[64,4,512]{2,1,0:T(4,128)S(1)}, u32[]{:S(2)}, u32[]{:S(2)}) async-start(f32[64,4,512]{2,1,0:T(4,128)} %broadcast_in_dim.18), calls=%async_computation.5 | async-start | bytes 1048576 | tf_op jit(solution)/shard_map/all_to_all | solution.py:19
  208.8 11.7 %cholesky.104 = f32[128,128]{1,0:T(8,128)S(1)} custom-call(f32[128,128]{1,0:T(8,128)S(1)} %cholesky.266), custom_call_target="Cholesky" | custom-call | tf_op jit(solution)/shard_map/jit(cholesky)/cholesky | solution.py:104
  220.6 9.8 %custom-call.31 = f32[1,128,128]{1,2,0:T(8,128)S(1)} custom-call(f32[1,128,128]{2,1,0:T(8,128)S(1)} %get-tuple-element.30), custom_call_target="InvertDiagBlocksLowerTriangular" | custom-call | tf_op jit(solution)/shard_map/jit(cholesky)/cholesky | solution.py:104
  231.1 11.7 %cholesky.217 = f32[128,128]{1,0:T(8,128)S(1)} custom-call(f32[128,128]{1,0:T(8,128)S(1)} %cholesky.270), custom_call_target="Cholesky" | custom-call | tf_op jit(solution)/shard_map/jit(cholesky)/cholesky | solution.py:104
  242.9 10.0 %custom-call.32 = f32[1,128,128]{1,2,0:T(8,128)S(1)} custom-call(f32[1,128,128]{2,1,0:T(8,128)S(1)} %get-tuple-element.27), custom_call_target="InvertDiagBlocksLowerTriangular" | custom-call | tf_op jit(solution)/shard_map/jit(cholesky)/cholesky | solution.py:104
  253.5 11.7 %cholesky.238 = f32[128,128]{1,0:T(8,128)S(1)} custom-call(f32[128,128]{1,0:T(8,128)S(1)} %cholesky.275), custom_call_target="Cholesky" | custom-call | tf_op jit(solution)/shard_map/jit(cholesky)/cholesky | solution.py:104
  266.0 9.8 %custom-call.33 = f32[1,128,128]{1,2,0:T(8,128)S(1)} custom-call(f32[1,128,128]{2,1,0:T(8,128)S(1)} %get-tuple-element.24), custom_call_target="InvertDiagBlocksLowerTriangular" | custom-call | tf_op jit(solution)/shard_map/jit(cholesky)/cholesky | solution.py:104
  276.4 11.9 %cholesky.255 = f32[128,128]{1,0:T(8,128)S(1)} custom-call(f32[128,128]{1,0:T(8,128)S(1)} %convolution_subtract_fusion.2), custom_call_target="Cholesky" | custom-call | tf_op jit(solution)/shard_map/jit(cholesky)/cholesky | solution.py:104
  292.3 8.5 %while.1 = (s32[]{:T(128)}, f32[512,512]{1,0:T(8,128)S(1)}, s32[4,2]{0,1:T(2,128)S(1)}, f32[4,128,128]{2,1,0:T(8,128)S(1)}, s32[]{:T(128)}) while((s32[]{:T(128)}, f32[512,512]{1,0:T(8,128)S(1)}, s32[4,2]{0,1:T(2,128)S(1)}, f32[4,128,128]{2,1,0:T(8,128)S(1)}, s32[]{:T(128)}) %tuple.31), condition=%wide.while_cond, body=%wide.while_body.sunk | while | flops 2 | bytes 131181 | solution.py:105
  300.8 39.3 %custom-call.34 = f32[4,128,128]{1,2,0:T(8,128)S(1)} custom-call(f32[4,128,128]{2,1,0:T(8,128)S(1)} %get-tuple-element.10), custom_call_target="InvertDiagBlocksLowerTriangular" | custom-call | tf_op jit(solution)/shard_map/jit(_solve_triangular)/triangular_solve | solution.py:105
  342.0 17.5 %all_to_all.63 = f32[8,64,512]{2,1,0:T(8,128)S(1)} all-to-all(f32[8,64,512]{2,1,0:T(8,128)S(1)} %broadcast_in_dim.20), channel_id=1, replica_groups=mesh['wide_0'=4,'wide_1'=4,'narrow_0'=4,'narrow_1'=2] {'narrow_0','narro..., dimensions={0} | all-to-all | bytes 2097152 | tf_op jit(solution)/shard_map/all_to_all | solution.py:19
  359.5 8.4 %fusion.34 = f32[2048,512]{1,0:T(8,128)} fusion(f32[512,2048]{1,0:T(8,128)S(1)} %copy-done.1, f32[512,512]{1,0:T(8,128)S(1)} %bitcast.78), kind=kOutput, calls=%fused_computation.78 | convolution fusion | flops 6442450944 | bytes 9437184 | tf_op jit(solution)/shard_map/dot_general | solution.py:108
  367.9 47.4 %reduce-scatter.3.cloned.1.call-done = f32[512,512]{1,0:T(8,128)} async-done(((f32[2048,512]{1,0:T(8,128)}), f32[512,512]{1,0:T(8,128)}) %reduce-scatter.3.cloned.1.call-update) | async-done | bytes 1048592 | tf_op jit(solution)/shard_map/reduce_scatter | solution.py:71
  415.3 25.1 %reduce-scatter.5.cloned.1.call-done = f32[128,512]{1,0:T(8,128)} async-done(((f32[512,512]{1,0:T(8,128)}), f32[128,512]{1,0:T(8,128)}) %reduce-scatter.5.cloned.1.call-update) | async-done | bytes 262160 | tf_op jit(solution)/shard_map/reduce_scatter | solution.py:71
  445.2 15.6 %all_to_all.65 = f32[64,1,512]{2,1,0:T(1,128)S(1)} all-to-all(f32[64,1,512]{2,1,0:T(1,128)S(1)} %broadcast_in_dim.22), channel_id=1, replica_groups=mesh['wide_0'=4,'wide_1'=4,'narrow_0'=4,'narrow_1'=2] {'wide_0','wide_1'..., dimensions={0} | all-to-all | bytes 262144 | tf_op jit(solution)/shard_map/all_to_all | solution.py:19
  464.3 8.4 %all-to-all-start.8 = ((f32[16,128,512]{2,1,0:T(8,128)}), f32[16,128,512]{2,1,0:T(8,128)}, u32[]{:S(2)}, u32[]{:S(2)}) async-start(f32[16,128,512]{2,1,0:T(8,128)} %stack.2), calls=%async_computation.10 | async-start | bytes 8388608 | tf_op jit(solution)/shard_map/all_to_all | solution.py:121
  472.8 58.4 %all-to-all-done.8 = f32[16,128,512]{2,1,0:T(8,128)} async-done(((f32[16,128,512]{2,1,0:T(8,128)}), f32[16,128,512]{2,1,0:T(8,128)}, u32[]{:S(2)}, u32[]{:S(2)}) %all-to-all-start.8) | async-done | bytes 4194336 | tf_op jit(solution)/shard_map/all_to_all | solution.py:121
  534.2 8.1 %multiply_convert_fusion = bf16[512,2048]{1,0:T(8,128)(2,1)} fusion(f32[512,512]{1,0:T(8,128)S(1)} %bitcast.79, f32[2048,512]{1,0:T(8,128)S(1)} %bitcast.82), kind=kOutput, calls=%fused_computation.2 | convolution fusion | flops 6444548096 | bytes 7340032 | tf_op jit(solution)/shard_map/dot_general | solution.py:133
  542.4 10.1 %multiply_subtract_fusion = f32[512,2048]{1,0:T(8,128)} fusion(f32[512,2048]{1,0:T(8,128)S(1)} %copy-done.2, f32[512,512]{1,0:T(8,128)S(1)} %bitcast.80, f32[2048,512]{1,0:T(8,128)} %bitcast.22), kind=kOutput, calls=%fused_computation.3 | convolution fusion | flops 6444548096 | bytes 13631488 | tf_op jit(solution)/shard_map/dot_general | solution.py:123
  (86 shorter events, 69.1 us)
Async XLA Ops:
  7.2 113.8 %all-gather.2.cloned.1.call-start = ((), (), s32[]{:S(2)}) async-start(), calls=%async_computation.13 | async-start | bytes 17825792 | tf_op jit(solution)/shard_map/all_gather | solution.py:90
  120.9 14.4 %copy-start.3 = (f32[2048,512]{1,0:T(8,128)S(1)}, f32[2048,512]{1,0:T(8,128)}, u32[]{:S(2)}) copy-start(f32[2048,512]{1,0:T(8,128)} %param.7) | copy-start | bytes 12582916
  135.3 6.9 %copy-start = (f32[512,2048]{1,0:T(8,128)}, f32[512,2048]{1,0:T(8,128)S(1)}, u32[]{:S(2)}) copy-start(f32[512,2048]{1,0:T(8,128)S(1)} %convolution_add_fusion) | copy-start | bytes 12582916
  186.0 16.9 %all-to-all-start.5 = ((f32[64,4,512]{2,1,0:T(4,128)}), f32[64,4,512]{2,1,0:T(4,128)S(1)}, u32[]{:S(2)}, u32[]{:S(2)}) async-start(f32[64,4,512]{2,1,0:T(4,128)} %broadcast_in_dim.18), calls=%async_computation.5 | async-start | bytes 1048576 | tf_op jit(solution)/shard_map/all_to_all | solution.py:19
  196.2 219.1 %reduce-scatter.3.cloned.1.call-start = ((), (), s32[]{:S(2)}) async-start(), calls=%async_computation.14 | async-start | bytes 5242880 | tf_op jit(solution)/shard_map/reduce_scatter | solution.py:71
  340.1 19.4 %copy-start.1 = (f32[512,2048]{1,0:T(8,128)S(1)}, f32[512,2048]{1,0:T(8,128)}, u32[]{:S(2)}) copy-start(f32[512,2048]{1,0:T(8,128)} %copy-done) | copy-start | bytes 12582916
  367.9 72.5 %reduce-scatter.5.cloned.1.call-start = ((), (), s32[]{:S(2)}) async-start(), calls=%async_computation.15 | async-start | bytes 1310720 | tf_op jit(solution)/shard_map/reduce_scatter | solution.py:71
  464.3 66.9 %all-to-all-start.8 = ((f32[16,128,512]{2,1,0:T(8,128)}), f32[16,128,512]{2,1,0:T(8,128)}, u32[]{:S(2)}, u32[]{:S(2)}) async-start(f32[16,128,512]{2,1,0:T(8,128)} %stack.2), calls=%async_computation.10 | async-start | bytes 8388608 | tf_op jit(solution)/shard_map/all_to_all | solution.py:121
  534.2 8.1 %copy-start.2 = (f32[512,2048]{1,0:T(8,128)S(1)}, f32[512,2048]{1,0:T(8,128)}, u32[]{:S(2)}) copy-start(f32[512,2048]{1,0:T(8,128)} %copy-done) | copy-start | bytes 12582916
Sparse Core Ops, SparseCore 0:
  10.1 110.7 all-gather.1
  368.0 47.2 reduce-scatter.2
  417.9 22.5 reduce-scatter.4
